TPU v7x, 32 devices: a whole 2x2x4 slice. The times are simulated.
32 devices in a mesh: groups: 2 (over y), ep: 4 (over z), tp: 4 (over x, core).
Axes of the slice: x: 2, y: 2, z: 4, core: 2. Of those that a mesh axis runs over, the one named last changes fastest.
Arguments:
- tokens: bfloat16 [1024, 4096], P(('groups', 'ep'), 'tp'), parts along dimension 0, may hold values from -6 to 6
- routes: int32 [1024, 16], P(('groups', 'ep')), parts along dimension 0, may hold values from 0 to 63, all different within a row; in each aligned block of 128 rows (0 to 127, 128 to 255, ...) at most 64 rows name the same one
- gates: float32 [1024, 16], P(('groups', 'ep')), parts along dimension 0, may hold values from 0.02 to 0.12
- w_latent: bfloat16 [4096, 1024], P('tp'), may hold values from -0.09375 to 0.09375
- w_gate: bfloat16 [64, 1024, 2048], P('ep', None, 'tp'), may hold values from -0.1875 to 0.1875
- w_up: bfloat16 [64, 1024, 2048], P('ep', None, 'tp'), may hold values from -0.1875 to 0.1875
- w_out: bfloat16 [64, 2048, 1024], P('ep', 'tp'), may hold values from -0.125 to 0.125
- w_restore: bfloat16 [1024, 4096], P('tp'), may hold values from -0.1875 to 0.1875
Outputs:
- mixed: bfloat16 [1024, 4096], P(('groups', 'ep'), 'tp'), parts along dimension 0
There are 2 independent parts, one for each index of `groups`. A program takes and returns all parts, laid end to end along the dimension named above; an argument that names none is the same for every part. Nothing has to cross between parts.
Inputs may be any that keep to these rules, and one draw needn't show every extreme that they name: `routes`: each row names 16 different experts. Within the rows of one device (aligned blocks of 128 rows) no expert is named by more than 64 rows, a bound that some block reaches.
All inputs are finite; a program needn't handle non-finite values.
Results may differ from a plain program's by a relative error of at most 0.025.
Values may be sent and summed in bfloat16 or wider, within the bound.
A program may use at most 192 MiB of HBM per device.

v0:
```python
import jax
import jax.numpy as jnp
from jax import lax
from jax.sharding import PartitionSpec as P

EXPERTS = 64
CAP = 64


def shards(tokens, routes, gates, w_latent, w_gate, w_up, w_out, w_restore):
    tok_rows = tokens.shape[0]
    chosen = routes.shape[1]
    exp_local = w_gate.shape[0]
    ep_count = lax.axis_size("ep")
    partial_value = jnp.dot(tokens, w_latent, preferred_element_type=jnp.float32)
    flat_routes = routes.reshape(-1)
    onehot = (flat_routes[:, None] == jnp.arange(EXPERTS, dtype=jnp.int32)[None, :]).astype(
        jnp.int32
    )
    ranks = jnp.sum((jnp.cumsum(onehot, axis=0) - onehot) * onehot, axis=1)
    slots = flat_routes * CAP + ranks
    latent_part = lax.psum_scatter(
        partial_value.astype(jnp.bfloat16), "tp", scatter_dimension=1, tiled=True
    )
    width = latent_part.shape[1]
    repeated = jnp.repeat(latent_part, chosen, axis=0)
    buffer = jnp.zeros((EXPERTS * CAP, width), jnp.bfloat16).at[slots].set(repeated)
    arrived = lax.all_to_all(
        buffer.reshape(ep_count, exp_local * CAP, width),
        "ep",
        split_axis=0,
        concat_axis=0,
        tiled=True,
    )
    piece = lax.all_gather(arrived, "tp", axis=2, tiled=True)
    cols = piece.shape[2]
    piece_four = piece.reshape(ep_count, exp_local, CAP, cols)
    gate_acc = jnp.einsum("secl,elh->sech", piece_four, w_gate, preferred_element_type=jnp.float32)
    up_acc = jnp.einsum("secl,elh->sech", piece_four, w_up, preferred_element_type=jnp.float32)
    hidden = (jax.nn.silu(gate_acc) * up_acc).astype(jnp.bfloat16)
    expert_part = jnp.einsum("sech,ehl->secl", hidden, w_out, preferred_element_type=jnp.float32)
    expert_out = lax.psum_scatter(
        expert_part.astype(jnp.bfloat16), "tp", scatter_dimension=3, tiled=True
    )
    share = expert_out.shape[3]
    returned = lax.all_to_all(
        expert_out.reshape(ep_count, exp_local * CAP, share),
        "ep",
        split_axis=0,
        concat_axis=0,
        tiled=True,
    )
    picked = returned.reshape(EXPERTS * CAP, share)[slots]
    weighted = gates[:, :, None] * picked.reshape(tok_rows, chosen, share).astype(jnp.float32)
    combined = jnp.sum(weighted, axis=1).astype(jnp.bfloat16)
    restored = jnp.dot(combined, w_restore, preferred_element_type=jnp.float32)
    return lax.psum_scatter(restored.astype(jnp.bfloat16), "tp", scatter_dimension=1, tiled=True)


def solution(mesh):
    return jax.shard_map(
        shards,
        mesh=mesh,
        in_specs=(
            P(("groups", "ep"), "tp"),
            P(("groups", "ep"), None),
            P(("groups", "ep"), None),
            P("tp", None),
            P("ep", None, "tp"),
            P("ep", None, "tp"),
            P("ep", "tp", None),
            P("tp", None),
        ),
        out_specs=P(("groups", "ep"), "tp"),
        check_vma=False,
    )
```

profile of v0, /device:TPU:0, one launch (start us, length us, event | category | flops | bytes accessed | tf_op | source)
XLA Modules:
  0.0 361.3 jit_solution(6267881905066933189)
XLA Ops:
  6.5 3.0 convolution_convert_fusion.1
  9.5 0.0 all-gather.2.cloned.1.call-start
  9.6 0.8 copy.12
  10.4 0.1 eq.29
  10.5 0.1 eq.25
  10.5 0.7 broadcast_multiply_fusion
  11.3 18.1 %reduce-window.6 = s32[64,16,128]{2,1,0:T(8,128)S(1)} reduce-window(s32[64,16,128]{2,1,0:T(8,128)S(1)} %fusion.30, s32[]{:T(128)} %constant.8.clone.1), window={size=1x1x128 pad=0_0x0_0x127_0}, to_apply=%region_0.0 | reduce-window | flops 16646144 | bytes 1048580 | tf_op jit(solution)/shard_map/reduce-window
  29.4 0.2 slice.10
  29.6 0.4 copy.21
  30.1 0.2 reduce-window.9
  30.3 0.2 broadcast_add_fusion
  30.5 0.1 copy.11
  30.6 0.1 mul.37
  30.7 0.3 fusion.29
  31.0 1.7 reduce-scatter.4.cloned.1.call-done
  32.7 0.9 broadcast_in_dim.5
  33.6 10.9 %scatter_custom_fusion = bf16[4096,256]{1,0:T(8,128)(2,1)} fusion(s32[2048]{0:T(1024)S(1)} %bitcast.83, bf16[2048,256]{1,0:T(8,128)(2,1)S(1)} %bitcast.79, bf16[]{:T(256)} %constant.6.clone.1), kind=kCustom, calls=%fused_computation.23 | custom fusion | bytes 2097154 | tf_op jit(solution)/shard_map/scatter | solution.py:27
  44.5 52.9 %all_to_all.10 = bf16[4,1024,256]{2,1,0:T(8,128)(2,1)} all-to-all(bf16[4,1024,256]{2,1,0:T(8,128)(2,1)} %bitcast.77), channel_id=1, replica_groups=mesh['groups'=2,'ep'=4,'tp'=4] {'ep'}, dimensions={0} | all-to-all | bytes 4194304 | tf_op jit(solution)/shard_map/all_to_all | solution.py:28
  97.4 0.0 all-gather.2.cloned.1.call-update
  97.5 0.0 reduce-scatter.6.cloned.1.call-start
  97.5 58.7 %all-gather.2.cloned.1.call-done = bf16[4,1024,1024]{2,1,0:T(8,128)(2,1)} async-done(((bf16[4,1024,256]{2,1,0:T(8,128)(2,1)}), bf16[4,1024,1024]{2,1,0:T(8,128)(2,1)}) %all-gather.2.cloned.1.call-update) | async-done | bytes 8388624 | tf_op jit(solution)/shard_map/all_gather | solution.py:35
  156.3 15.9 %fusion.4 = f32[16,4,64,512]{3,2,1,0:T(8,128)} fusion(bf16[16,1024,512]{2,1,0:T(8,128)(2,1)} %param.12, bf16[4,16,64,1024]{3,2,1,0:T(8,128)(2,1)} %bitcast.85), kind=kOutput, calls=%fused_computation.6 | convolution fusion | flops 4294967296 | bytes 33554432 | tf_op jit(solution)/shard_map/secl,elh->sech/dot_general | solution.py:38
  172.1 20.9 %convert_bitcast_fusion = bf16[4,16,64,1024]{3,2,0,1:T(8,128)(2,1)} fusion(bf16[16,512,1024]{2,1,0:T(8,128)(2,1)} %param.14, f32[16,4,64,512]{3,2,1,0:T(8,128)} %fusion.4, bf16[16,1024,512]{2,1,0:T(8,128)(2,1)} %param.13, bf16[4,16,64,1024]{3,2,1,0:T(8,128)(2,1)} %bitcast.86), kind=kOutput, calls=%fused_computation.15 | convolution fusion | flops 8606711808 | bytes 58720256 | tf_op jit(solution)/shard_map/sech,ehl->secl/dot_general | solution.py:41
  193.1 71.9 %reduce-scatter.6.cloned.1.call-done = bf16[4,16,64,256]{3,2,0,1:T(8,128)(2,1)} async-done(((bf16[4,16,64,1024]{3,2,0,1:T(8,128)(2,1)}), bf16[4,16,64,256]{3,2,0,1:T(8,128)(2,1)}) %reduce-scatter.6.cloned.1.call-update) | async-done | bytes 2097168 | tf_op jit(solution)/shard_map/reduce_scatter | solution.py:42
  264.9 3.1 copy.17
  268.0 4.6 %all-to-all-start.1 = ((bf16[4,1024,256]{2,1,0:T(8,128)(2,1)}), bf16[4,1024,256]{2,1,0:T(8,128)(2,1)}, u32[]{:S(2)}, u32[]{:S(2)}) async-start(bf16[4,1024,256]{2,1,0:T(8,128)(2,1)} %bitcast.76), calls=%async_computation.3 | async-start | bytes 4194304 | tf_op jit(solution)/shard_map/all_to_all | solution.py:46
  272.7 0.1 copy.10
  272.8 48.3 %all-to-all-done.1 = bf16[4,1024,256]{2,1,0:T(8,128)(2,1)} async-done(((bf16[4,1024,256]{2,1,0:T(8,128)(2,1)}), bf16[4,1024,256]{2,1,0:T(8,128)(2,1)}, u32[]{:S(2)}, u32[]{:S(2)}) %all-to-all-start.1) | async-done | bytes 2097184 | tf_op jit(solution)/shard_map/all_to_all | solution.py:46
  321.0 8.5 %gather_fusion = bf16[2048,256]{1,0:T(8,128)(2,1)S(1)} fusion(bf16[4096,256]{1,0:T(8,128)(2,1)} %bitcast.18, s32[2048]{0:T(1024)S(1)} %broadcast_clamp_fusion), kind=kCustom, calls=%fused_computation | custom fusion | bytes 2105344 | tf_op jit(solution)/shard_map/gather | solution.py:53
  329.5 0.6 fusion.24
  330.1 1.4 convolution_convert_fusion
  331.6 23.2 %reduce-scatter.8.cloned.1.call-done = bf16[128,1024]{1,0:T(8,128)(2,1)} async-done(((bf16[128,4096]{1,0:T(8,128)(2,1)}), bf16[128,1024]{1,0:T(8,128)(2,1)}) %reduce-scatter.8.cloned.1.call-update) | async-done | bytes 262160 | tf_op jit(solution)/shard_map/reduce_scatter | solution.py:57
  (12 shorter events, 0.1 us)
Async XLA Ops:
  6.5 323.6 %copy-start = (bf16[256,4096]{1,0:T(8,128)(2,1)S(1)}, bf16[256,4096]{1,0:T(8,128)(2,1)}, u32[]{:S(2)}) copy-start(bf16[256,4096]{1,0:T(8,128)(2,1)} %param.15) | copy-start | bytes 6291460
  6.5 26.1 %reduce-scatter.4.cloned.1.call-start = ((), (), s32[]{:S(2)}) async-start(), calls=%async_computation.5 | async-start | bytes 327680 | tf_op jit(solution)/shard_map/reduce_scatter | solution.py:22
  9.5 146.7 %all-gather.2.cloned.1.call-start = ((), (), s32[]{:S(2)}) async-start(), calls=%async_computation.6 | async-start | bytes 10485760 | tf_op jit(solution)/shard_map/all_gather | solution.py:35
  97.5 167.4 %reduce-scatter.6.cloned.1.call-start = ((), (), s32[]{:S(2)}) async-start(), calls=%async_computation.7 | async-start | bytes 10485760 | tf_op jit(solution)/shard_map/reduce_scatter | solution.py:42
  193.0 79.6 %copy-start.1 = (f32[128,16]{0,1:T(8,128)S(1)}, f32[128,16]{0,1:T(8,128)}, u32[]{:S(2)}) copy-start(f32[128,16]{0,1:T(8,128)} %param.10) | copy-start | bytes 24580
  268.0 53.0 %all-to-all-start.1 = ((bf16[4,1024,256]{2,1,0:T(8,128)(2,1)}), bf16[4,1024,256]{2,1,0:T(8,128)(2,1)}, u32[]{:S(2)}, u32[]{:S(2)}) async-start(bf16[4,1024,256]{2,1,0:T(8,128)(2,1)} %bitcast.76), calls=%async_computation.3 | async-start | bytes 4194304 | tf_op jit(solution)/shard_map/all_to_all | solution.py:46
  272.7 82.1 %reduce-scatter.8.cloned.1.call-start = ((), (), s32[]{:S(2)}) async-start(), calls=%async_computation.8 | async-start | bytes 1310720 | tf_op jit(solution)/shard_map/reduce_scatter | solution.py:57
Sparse Core Ops, SparseCore 0:
  9.8 22.8 reduce-scatter.3
  97.6 58.6 all-gather.1
  193.2 71.6 reduce-scatter.5
  331.7 23.0 reduce-scatter.7
where the time goes:
time: 362 us; the launch traced here: 361 us
  waiting for transfers between devices  204 us (56%)
  blocking collectives  52.9 us (15%)
  matrix products  41.2 us (11%)
  local copies, waits for them, and re-layouts  25.4 us (7%)
  other arithmetic  20.1 us (6%)
  between operations  13.2 us (4%)
  starting transfers between devices  4.69 us (1%)
    reduce_scatter x1, waiting for transfers between devices, shards(): lax.psum_scatter(expert_part.astype(jnp.bfloat16), 'tp', scatter_dimensio...  71.9 us
    all_gather x1, waiting for transfers between devices, shards(): piece = lax.all_gather(arrived, 'tp', axis=2, tiled=True)  58.7 us
    all_to_all x1, blocking collectives, shards(): lax.all_to_all(buffer.reshape(ep_count, exp_local * CAP, width), 'ep', sp...  52.9 us
    all_to_all x1, waiting for transfers between devices, shards(): lax.all_to_all(expert_out.reshape(ep_count, exp_local * CAP, share), 'ep'...  48.3 us
    reduce_scatter x1, waiting for transfers between devices, shards(): lax.psum_scatter(restored.astype(jnp.bfloat16), 'tp', scatter_dimension=1...  23.2 us
    dot_general x1, matrix products, shards(): jnp.einsum('sech,ehl->secl', hidden, w_out, preferred_element_type=jnp.fl...  20.9 us
    another operation x3, other arithmetic  18.5 us
    dot_general x1, matrix products, shards(): jnp.einsum('secl,elh->sech', piece_four, w_gate, preferred_element_type=j...  15.9 us
  transfers between devices with their start and end apart: 5, of which 5 were waited for; matrix products, arithmetic and copies ran while one was open for 6% of the time, Pallas kernels for 0%

commit v1 on v0

v1 whole, which is shorter than its diff:
```python
import jax
import jax.numpy as jnp
from jax import lax
from jax.experimental import pallas as pl
from jax.experimental.pallas import tpu as pltpu
from jax.sharding import PartitionSpec as P


def ffn_kernel(lat_ref, routes_ref, gates_ref, ids_ref, wg_ref, wu_ref, wo_ref, out_ref, acc_ref):
    step = pl.program_id(0)
    count = pl.num_programs(0)
    rows = lat_ref.shape[0]
    tile = min(rows, 256)
    expert = ids_ref[0] + step

    @pl.when(step == 0)
    def _():
        acc_ref[...] = jnp.zeros_like(acc_ref)

    def body(i, carry):
        r = pl.ds(pl.multiple_of(i * tile, tile), tile)
        x = lat_ref[r, :]
        weight = jnp.sum(jnp.where(routes_ref[r, :] == expert, gates_ref[r, :], 0.0), axis=1, keepdims=True)
        g = jnp.dot(x, wg_ref[0], preferred_element_type=jnp.float32)
        u = jnp.dot(x, wu_ref[0], preferred_element_type=jnp.float32)
        h = (g / (1.0 + jnp.exp(-g)) * u * weight).astype(jnp.bfloat16)
        acc_ref[r, :] += jnp.dot(h, wo_ref[0], preferred_element_type=jnp.float32)
        return carry

    lax.fori_loop(0, rows // tile, body, 0)

    @pl.when(step == count - 1)
    def _():
        out_ref[...] = acc_ref[...].astype(out_ref.dtype)


def ffn(lat, routes, gates, first, wg, wu, wo):
    rows, width = lat.shape
    count, _, hidden = wg.shape
    top = routes.shape[1]
    whole = lambda *shape: pl.BlockSpec(shape, lambda e: (0,) * len(shape))
    return pl.pallas_call(
        ffn_kernel,
        grid=(count,),
        out_shape=jax.ShapeDtypeStruct((rows, width), jnp.bfloat16),
        in_specs=[
            whole(rows, width),
            whole(rows, top),
            whole(rows, top),
            pl.BlockSpec(memory_space=pltpu.SMEM),
            pl.BlockSpec((1, width, hidden), lambda e: (e, 0, 0)),
            pl.BlockSpec((1, width, hidden), lambda e: (e, 0, 0)),
            pl.BlockSpec((1, hidden, width), lambda e: (e, 0, 0)),
        ],
        out_specs=whole(rows, width),
        scratch_shapes=[pltpu.VMEM((rows, width), jnp.float32)],
        compiler_params=pltpu.CompilerParams(vmem_limit_bytes=56 * 1024 * 1024),
    )(lat, routes, gates, first, wg, wu, wo)


def shards(tokens, routes, gates, w_latent, w_gate, w_up, w_out, w_restore):
    count = w_gate.shape[0]
    partial_value = jnp.dot(tokens, w_latent, preferred_element_type=jnp.float32)
    routes_all = lax.all_gather(routes, "ep", axis=0, tiled=True)
    gates_all = lax.all_gather(gates, "ep", axis=0, tiled=True)
    latent_part = lax.psum_scatter(
        partial_value.astype(jnp.bfloat16), "tp", scatter_dimension=1, tiled=True
    )
    lat = lax.all_gather(latent_part, "ep", axis=0, tiled=True)
    lat = lax.all_gather(lat, "tp", axis=1, tiled=True)
    first = (lax.axis_index("ep") * count).astype(jnp.int32).reshape(1)
    part = ffn(lat, routes_all, gates_all, first, w_gate, w_up, w_out)
    part = lax.psum_scatter(part, "tp", scatter_dimension=1, tiled=True)
    combined = lax.psum_scatter(part, "ep", scatter_dimension=0, tiled=True)
    restored = jnp.dot(combined, w_restore, preferred_element_type=jnp.float32)
    return lax.psum_scatter(restored.astype(jnp.bfloat16), "tp", scatter_dimension=1, tiled=True)


def solution(mesh):
    return jax.shard_map(
        shards,
        mesh=mesh,
        in_specs=(
            P(("groups", "ep"), "tp"),
            P(("groups", "ep"), None),
            P(("groups", "ep"), None),
            P("tp", None),
            P("ep", None, "tp"),
            P("ep", None, "tp"),
            P("ep", "tp", None),
            P("tp", None),
        ),
        out_specs=P(("groups", "ep"), "tp"),
        check_vma=False,
    )
```

time: 362 us -> 196 us (0.54)
  waiting for transfers between devices: 204 us -> 92.5 us
  Pallas kernels: 0 us -> 38.7 us
  matrix products: 41.2 us -> 5.23 us
  local copies, waits for them, and re-layouts: 25.4 us -> 0.21 us
  other arithmetic: 20.1 us -> 0 us
  blocking collectives: 52.9 us -> 45.7 us
  starting transfers between devices: 4.69 us -> 0.17 us
    all_gather x1, waiting for transfers between devices: 58.7 us -> 0.01 us  [shards(): lat = lax.all_gather(lat, 'tp', axis=1, tiled=True)]
    all_to_all x1 -> x0, blocking collectives: 52.9 us -> none  [shards(): lax.all_to_all(buffer.reshape(ep_count, exp_local * CAP, width), 'ep', sp...]
    all_to_all x1 -> x0, waiting for transfers between devices: 48.3 us -> none  [shards(): lax.all_to_all(expert_out.reshape(ep_count, exp_local * CAP, share), 'ep'...]
    all_gather x0 -> x3, blocking collectives: none -> 45.7 us  [the longest x1 15.8 us: shards(): lat = lax.all_gather(latent_part, 'ep', axis=0, tiled=True)]
    pallas_call x0 -> x1, Pallas kernels: none -> 38.7 us  [ffn(): pl.pallas_call(ffn_kernel, grid=(count,), out_shape=jax.ShapeDtypeStruct(...]
    dot_general x2 -> x0, matrix products: 36.8 us -> none  [the longest x1 20.9 us: shards(): jnp.einsum('sech,ehl->secl', hidden, w_out, preferred_element_type=jnp.fl...]
    reduce_scatter x1 -> x2, waiting for transfers between devices: 71.9 us -> 46 us  [the longest x1 24.3 us: shards(): part = lax.psum_scatter(part, 'tp', scatter_dimension=1, tiled=True)]
    reduce_scatter x1, waiting for transfers between devices: 1.71 us -> 23 us  [shards(): lax.psum_scatter(partial_value.astype(jnp.bfloat16), 'tp', scatter_dimens...]
  transfers between devices with their start and end apart: 5 -> 5, of which waited for: 5 -> 4; matrix products, arithmetic and copies ran while one was open for 6% -> 0% of each run, Pallas kernels for 0% -> 0%
where the time goes in v1:
time: 196 us
  waiting for transfers between devices  92.5 us (47%)
  blocking collectives  45.7 us (23%)
  Pallas kernels  38.7 us (20%)
  between operations  13.2 us (7%)
  matrix products  5.23 us (3%)
    pallas_call x1, Pallas kernels, ffn(): pl.pallas_call(ffn_kernel, grid=(count,), out_shape=jax.ShapeDtypeStruct(...  38.7 us
    reduce_scatter x1, waiting for transfers between devices, shards(): part = lax.psum_scatter(part, 'tp', scatter_dimension=1, tiled=True)  24.3 us
    reduce_scatter x1, waiting for transfers between devices, shards(): lax.psum_scatter(restored.astype(jnp.bfloat16), 'tp', scatter_dimension=1...  23.4 us
    reduce_scatter x1, waiting for transfers between devices, shards(): lax.psum_scatter(partial_value.astype(jnp.bfloat16), 'tp', scatter_dimens...  23 us
    reduce_scatter x1, waiting for transfers between devices, shards(): combined = lax.psum_scatter(part, 'ep', scatter_dimension=0, tiled=True)  21.7 us
    all_gather x1, blocking collectives, shards(): lat = lax.all_gather(latent_part, 'ep', axis=0, tiled=True)  15.8 us
    all_gather x1, blocking collectives, shards(): gates_all = lax.all_gather(gates, 'ep', axis=0, tiled=True)  15.2 us
    all_gather x1, blocking collectives, shards(): routes_all = lax.all_gather(routes, 'ep', axis=0, tiled=True)  14.7 us
  transfers between devices with their start and end apart: 5, of which 4 were waited for; matrix products, arithmetic and copies ran while one was open for 0% of the time, Pallas kernels for 0%

profile of v1, /device:TPU:0, one launch (start us, length us, event | category | flops | bytes accessed | tf_op | source)
XLA Modules:
  0.0 195.6 jit_solution(10955263634292515977)
XLA Ops:
  6.5 0.0 copy-start
  6.5 0.0 copy-start.1
  6.5 0.0 copy-start.2
  6.5 0.0 reduce-scatter.5.cloned.1.call-start
  6.5 3.0 %convolution_convert_fusion.1 = bf16[128,1024]{1,0:T(8,128)(2,1)} fusion(bf16[128,1024]{1,0:T(8,128)(2,1)} %param.8, bf16[1024,1024]{1,0:T(8,128)(2,1)} %param.11), kind=kOutput, calls=%fused_computation.1 | convolution fusion | flops 268566528 | bytes 2621440 | tf_op jit(solution)/shard_map/dot_general | solution.py:63
  9.5 0.0 reduce-scatter.5.cloned.1.call-update
  9.5 0.0 all-gather.2.cloned.1.call-start
  9.6 23.0 %reduce-scatter.5.cloned.1.call-done = bf16[128,256]{1,0:T(8,128)(2,1)} async-done(((bf16[128,1024]{1,0:T(8,128)(2,1)}), bf16[128,256]{1,0:T(8,128)(2,1)}) %reduce-scatter.5.cloned.1.call-update) | async-done | bytes 65552 | tf_op jit(solution)/shard_map/reduce_scatter | solution.py:66
  32.6 15.8 %all_gather.12 = bf16[512,256]{1,0:T(8,128)(2,1)} all-gather(bf16[128,256]{1,0:T(8,128)(2,1)} %reduce-scatter.5.cloned.1.call-done), channel_id=1, replica_groups=mesh['groups'=2,'ep'=4,'tp'=4] {'ep'}, dimensions={0}, use_global_device_ids=true | all-gather | bytes 327680 | tf_op jit(solution)/shard_map/all_gather | solution.py:69
  48.4 0.0 all-gather.2.cloned.1.call-update
  48.4 0.0 reduce-scatter.7.cloned.1.call-start
  48.5 0.0 copy-done.1
  48.5 0.1 copy.9
  48.6 0.0 copy-done.2
  48.6 0.1 copy.10
  48.7 15.2 %all_gather.15.gates_ref = f32[512,16]{1,0:T(8,128)} all-gather(f32[128,16]{1,0:T(8,128)S(1)} %copy.10), channel_id=1, replica_groups=mesh['groups'=2,'ep'=4,'tp'=4] {'ep'}, dimensions={0}, use_global_device_ids=true | all-gather | bytes 40960 | tf_op jit(solution)/shard_map/all_gather | solution.py:65
  63.9 14.7 %all_gather.14.routes_ref = s32[512,16]{1,0:T(8,128)} all-gather(s32[128,16]{1,0:T(8,128)S(1)} %copy.9), channel_id=1, replica_groups=mesh['groups'=2,'ep'=4,'tp'=4] {'ep'}, dimensions={0}, use_global_device_ids=true | all-gather | bytes 40960 | tf_op jit(solution)/shard_map/all_gather | solution.py:64
  78.5 0.0 all-gather.2.cloned.1.call-done.lat_ref
  78.5 38.7 %shard_map.82 = bf16[512,1024]{1,0:T(8,128)(2,1)} custom-call(bf16[512,1024]{1,0:T(8,128)(2,1)} %all-gather.2.cloned.1.call-done.lat_ref, s32[512,16]{1,0:T(8,128)} %all_gather.14.routes_ref, f32[512,16]{1,0:T(8,128)} %all_gather.15.gates_ref, s32[1]{0:T(128)} %bitcast.ids_ref, bf16[16,1024,512]{2,1,0:T(8,128)(2,1)} %wg_ref.1, ...), custom_call_target="tpu_custom_call" | custom-call | tf_op jit(solution)/shard_map/pallas_call | solution.py:42
  117.2 0.0 reduce-scatter.7.cloned.1.call-update
  117.2 0.0 reduce-scatter.9.cloned.1.call-start
  117.3 24.3 %reduce-scatter.7.cloned.1.call-done = bf16[512,256]{1,0:T(8,128)(2,1)} async-done(((bf16[512,1024]{1,0:T(8,128)(2,1)}), bf16[512,256]{1,0:T(8,128)(2,1)}) %reduce-scatter.7.cloned.1.call-update) | async-done | bytes 262160 | tf_op jit(solution)/shard_map/reduce_scatter | solution.py:73
  141.6 0.0 reduce-scatter.9.cloned.1.call-update
  141.6 0.0 reduce-scatter.11.cloned.1.call-start
  141.6 21.7 %reduce-scatter.9.cloned.1.call-done = bf16[128,256]{1,0:T(8,128)(2,1)} async-done(((bf16[512,256]{1,0:T(8,128)(2,1)}), bf16[128,256]{1,0:T(8,128)(2,1)}) %reduce-scatter.9.cloned.1.call-update) | async-done | bytes 65552 | tf_op jit(solution)/shard_map/reduce_scatter | solution.py:74
  163.4 0.0 copy-done
  163.4 2.3 %convolution_convert_fusion = bf16[128,4096]{1,0:T(8,128)(2,1)} fusion(bf16[128,256]{1,0:T(8,128)(2,1)} %reduce-scatter.9.cloned.1.call-done, bf16[256,4096]{1,0:T(8,128)(2,1)S(1)} %copy-done), kind=kOutput, calls=%fused_computation | convolution fusion | flops 268959744 | bytes 3211264 | tf_op jit(solution)/shard_map/dot_general | solution.py:75
  165.6 0.0 reduce-scatter.11.cloned.1.call-update
  165.7 23.4 %reduce-scatter.11.cloned.1.call-done = bf16[128,1024]{1,0:T(8,128)(2,1)} async-done(((bf16[128,4096]{1,0:T(8,128)(2,1)}), bf16[128,1024]{1,0:T(8,128)(2,1)}) %reduce-scatter.11.cloned.1.call-update) | async-done | bytes 262160 | tf_op jit(solution)/shard_map/reduce_scatter | solution.py:76
Async XLA Ops:
  6.5 156.8 %copy-start = (bf16[256,4096]{1,0:T(8,128)(2,1)S(1)}, bf16[256,4096]{1,0:T(8,128)(2,1)}, u32[]{:S(2)}) copy-start(bf16[256,4096]{1,0:T(8,128)(2,1)} %param.15) | copy-start | bytes 6291460
  6.5 41.9 %copy-start.1 = (s32[128,16]{0,1:T(8,128)S(1)}, s32[128,16]{0,1:T(8,128)}, u32[]{:S(2)}) copy-start(s32[128,16]{0,1:T(8,128)} %param.9) | copy-start | bytes 24580
  6.5 42.0 %copy-start.2 = (f32[128,16]{0,1:T(8,128)S(1)}, f32[128,16]{0,1:T(8,128)}, u32[]{:S(2)}) copy-start(f32[128,16]{0,1:T(8,128)} %param.10) | copy-start | bytes 24580
  6.5 26.0 %reduce-scatter.5.cloned.1.call-start = ((), (), s32[]{:S(2)}) async-start(), calls=%async_computation.4 | async-start | bytes 327680 | tf_op jit(solution)/shard_map/reduce_scatter | solution.py:66
  9.5 69.0 %all-gather.2.cloned.1.call-start = ((), (), s32[]{:S(2)}) async-start(), calls=%async_computation.5 | async-start | bytes 1310720 | tf_op jit(solution)/shard_map/all_gather | solution.py:70
  48.4 93.2 %reduce-scatter.7.cloned.1.call-start = ((), (), s32[]{:S(2)}) async-start(), calls=%async_computation.6 | async-start | bytes 1310720 | tf_op jit(solution)/shard_map/reduce_scatter | solution.py:73
  117.2 46.1 %reduce-scatter.9.cloned.1.call-start = ((), (), s32[]{:S(2)}) async-start(), calls=%async_computation.7 | async-start | bytes 327680 | tf_op jit(solution)/shard_map/reduce_scatter | solution.py:74
  141.6 47.4 %reduce-scatter.11.cloned.1.call-start = ((), (), s32[]{:S(2)}) async-start(), calls=%async_computation.8 | async-start | bytes 1310720 | tf_op jit(solution)/shard_map/reduce_scatter | solution.py:76
Sparse Core Ops, SparseCore 0:
  9.8 22.7 reduce-scatter.4
  48.5 15.9 all-gather.1
  117.4 24.1 reduce-scatter.6
  143.7 19.6 reduce-scatter.8
  165.9 23.1 reduce-scatter.10

commit v2 on v0

v2 whole, which is shorter than its diff:
```python
import functools

import jax
import jax.numpy as jnp
from jax import lax
from jax.experimental import pallas as pl
from jax.experimental.pallas import tpu as pltpu
from jax.sharding import PartitionSpec as P

F32, BF16 = jnp.float32, jnp.bfloat16
MESH = pl.DeviceIdType.MESH
SLOTS = 4


def remote(src, dst, send, recv, **where):
    return pltpu.make_async_remote_copy(
        src_ref=src, dst_ref=dst, send_sem=send, recv_sem=recv, device_id=where, device_id_type=MESH
    )


def layer(
    ep_n, tp_n, tok_ref, pack_ref, wl_ref, wg_hbm, wu_hbm, wo_hbm, wr_hbm, out_ref,
    p_send, p_recv, lat, pack, wg, wu, wo, wr, acc, r1_send, r1_recv, r2_send, r2_recv,
    r3_send, r3_recv, comb,
    p_sems, k_sems, a_sems, b1_sems, b2_sems, b3_sems, w_sems, wr_sems, own_sem,
    r1_sems, r2_sems, r3_sems, c_sems,
):
    ep, tp = lax.axis_index("ep"), lax.axis_index("tp")
    far = lax.rem(tp + 2, 4)
    near = tp + 1 - 2 * lax.rem(tp, 2)
    near_far = lax.rem(near + 2, 4)
    count = wg_hbm.shape[0]
    slots = wg.shape[0]
    toks, top = tok_ref.shape[0], pack_ref.shape[1] // 2
    rows, width = lat.shape
    quarter = width // tp_n
    out_cols = out_ref.shape[1]

    def cols(q):
        return pl.ds(pl.multiple_of(q * quarter, quarter), quarter)

    def block(b):
        return pl.ds(pl.multiple_of(b * toks, toks), toks)

    def loads(e, s):
        return [
            pltpu.make_async_copy(hbm.at[e], vmem.at[s], w_sems.at[s, i])
            for i, (hbm, vmem) in enumerate(((wg_hbm, wg), (wu_hbm, wu), (wo_hbm, wo)))
        ]

    for s in range(slots):
        for c in loads(s, s):
            c.start()

    barrier = pltpu.get_barrier_semaphore()
    for d in range(1, ep_n):
        pl.semaphore_signal(barrier, inc=1, device_id={"ep": lax.rem(ep + d, ep_n)}, device_id_type=MESH)
    for d in range(1, tp_n):
        pl.semaphore_signal(barrier, inc=1, device_id={"tp": lax.rem(tp + d, tp_n)}, device_id_type=MESH)
    pl.semaphore_wait(barrier, ep_n + tp_n - 2)

    sent = []

    parts = [None]
    for d in range(1, tp_n):
        peer = lax.rem(tp + d, tp_n)
        p_send[d] = jnp.dot(tok_ref[...], wl_ref[:, cols(peer)], preferred_element_type=F32).astype(BF16)
        c = remote(p_send.at[d], p_recv.at[d], p_sems.at[0, d], p_sems.at[1, d], tp=peer)
        c.start()
        parts.append(c)
        sent.append(c)
    mine = jnp.dot(tok_ref[...], wl_ref[:, cols(tp)], preferred_element_type=F32)
    packs = [None]
    pack[block(ep), :] = pack_ref[...]
    for d in range(1, ep_n):
        c = remote(
            pack_ref, pack.at[block(ep), :], k_sems.at[0, d], k_sems.at[1, d], ep=lax.rem(ep + d, ep_n)
        )
        c.start()
        packs.append(c)
        sent.append(c)
    for d in range(1, tp_n):
        parts[d].wait_recv()
        mine = mine + p_recv[d].astype(F32)
    lat[block(ep), cols(tp)] = mine.astype(BF16)

    own = lat.at[block(ep), cols(tp)]
    spread = [None]
    for d in range(1, ep_n):
        c = remote(own, own, a_sems.at[0, d], a_sems.at[1, d], ep=lax.rem(ep + d, ep_n))
        c.start()
        spread.append(c)
        sent.append(c)
    b1, b2, b3 = [], [], []
    for d in range(ep_n):
        if d:
            spread[d].wait_recv()
        piece = lat.at[block(lax.rem(ep + ep_n - d, ep_n)), cols(tp)]
        c = remote(piece, piece, b1_sems.at[0, d], b1_sems.at[1, d], tp=far)
        c.start()
        b1.append(c)
        c = remote(piece, piece, b2_sems.at[0, d], b2_sems.at[1, d], tp=near)
        c.start()
        b2.append(c)
    for d in range(ep_n):
        b1[d].wait_recv()
        piece = lat.at[block(lax.rem(ep + ep_n - d, ep_n)), cols(far)]
        c = remote(piece, piece, b3_sems.at[0, d], b3_sems.at[1, d], tp=near)
        c.start()
        b3.append(c)
    sent += b1 + b2 + b3
    for d in range(ep_n):
        b2[d].wait_recv()
        b3[d].wait_recv()
        if d:
            packs[d].wait_recv()

    restore = []
    for d in range(1, tp_n):
        peer = lax.rem(tp + d, tp_n)
        c = remote(
            wr_hbm.at[:, pl.ds(pl.multiple_of(peer * out_cols, out_cols), out_cols)],
            wr.at[cols(tp), :], wr_sems.at[0, d], wr_sems.at[1, d], tp=peer,
        )
        c.start()
        restore.append(c)
        sent.append(c)
    own_restore = pltpu.make_async_copy(
        wr_hbm.at[:, pl.ds(pl.multiple_of(tp * out_cols, out_cols), out_cols)], wr.at[cols(tp), :], own_sem
    )
    own_restore.start()

    acc[...] = jnp.zeros_like(acc)
    tile = min(rows, 256)
    pair = min(rows // tile, 2)

    def expert(e, carry):
        s = lax.rem(e, slots)
        for c in loads(e, s):
            c.wait()
        name = (ep * count + e).astype(F32)

        def tiles(i, inner):
            for j in range(pair):
                r = pl.ds(pl.multiple_of((i * pair + j) * tile, tile), tile)
                x = lat[r, :]
                chosen = pack[r, :]
                weight = jnp.sum(
                    jnp.where(chosen[:, :top] == name, chosen[:, top:], 0.0), axis=1, keepdims=True
                )
                g = jnp.dot(x, wg[s], preferred_element_type=F32)
                u = jnp.dot(x, wu[s], preferred_element_type=F32)
                h = (g / (1.0 + jnp.exp(-g)) * u * weight).astype(BF16)
                acc[r, :] += jnp.dot(h, wo[s], preferred_element_type=F32)
            return inner

        if rows == tile * pair:
            tiles(0, 0)
        else:
            lax.fori_loop(0, rows // (tile * pair), tiles, 0)

        @pl.when(e + slots < count)
        def _():
            for c in loads(e + slots, s):
                c.start()

        return carry

    lax.fori_loop(0, count, expert, 0)

    order = list(range(1, ep_n)) + [0]
    at = [block(lax.rem(ep + d, ep_n)) for d in range(ep_n)]
    r1, r2, r3 = {}, {}, {}
    for d in order:
        r1_send[d, 0] = acc[at[d], cols(near)].astype(BF16)
        r1_send[d, 1] = acc[at[d], cols(near_far)].astype(BF16)
        r1[d] = remote(r1_send.at[d], r1_recv.at[d], r1_sems.at[0, d], r1_sems.at[1, d], tp=near)
        r1[d].start()
    for d in order:
        r1[d].wait_recv()
        r2_send[d] = (acc[at[d], cols(far)] + r1_recv[d, 1].astype(F32)).astype(BF16)
        r2[d] = remote(r2_send.at[d], r2_recv.at[d], r2_sems.at[0, d], r2_sems.at[1, d], tp=far)
        r2[d].start()
    for d in order:
        r2[d].wait_recv()
        total = acc[at[d], cols(tp)] + r1_recv[d, 0].astype(F32) + r2_recv[d].astype(F32)
        if d:
            r3_send[d] = total.astype(BF16)
            r3[d] = remote(
                r3_send.at[d], r3_recv.at[d], r3_sems.at[0, d], r3_sems.at[1, d], ep=lax.rem(ep + d, ep_n)
            )
            r3[d].start()
    for d in range(1, ep_n):
        r3[d].wait_recv()
        total = total + r3_recv[d].astype(F32)
    sent += list(r1.values()) + list(r2.values()) + list(r3.values())
    comb[:, cols(tp)] = total.astype(BF16)
    gathered = []
    for d in range(1, tp_n):
        c = remote(
            comb.at[:, cols(tp)], comb.at[:, cols(tp)], c_sems.at[0, d], c_sems.at[1, d],
            tp=lax.rem(tp + d, tp_n),
        )
        c.start()
        gathered.append(c)
    sent += gathered
    own_restore.wait()
    for c in restore:
        c.wait_recv()
    for c in gathered:
        c.wait_recv()
    out_ref[...] = jnp.dot(comb[...], wr[...], preferred_element_type=F32).astype(out_ref.dtype)
    for c in sent:
        c.wait_send()


def solution(mesh):
    ep_n, tp_n = mesh.shape["ep"], mesh.shape["tp"]

    def shards(tokens, routes, gates, w_latent, w_gate, w_up, w_out, w_restore):
        toks = tokens.shape[0]
        count, width, hidden = w_gate.shape
        rows, quarter = toks * ep_n, width // tp_n
        out_cols = w_restore.shape[1] // tp_n
        slots = min(SLOTS, count)
        pack = jnp.concatenate([routes.astype(F32), gates], axis=1)
        vmem, dma = pltpu.VMEM, pltpu.SemaphoreType.DMA
        in_vmem, in_hbm = pl.BlockSpec(memory_space=pltpu.VMEM), pl.BlockSpec(memory_space=pl.ANY)
        work = 6 * rows * width * hidden * count
        return pl.pallas_call(
            functools.partial(layer, ep_n, tp_n),
            out_shape=jax.ShapeDtypeStruct((toks, out_cols), BF16),
            in_specs=[in_vmem] * 3 + [in_hbm] * 4,
            out_specs=in_vmem,
            scratch_shapes=[
                vmem((tp_n, toks, quarter), BF16),
                vmem((tp_n, toks, quarter), BF16),
                vmem((rows, width), BF16),
                vmem((rows, pack.shape[1]), F32),
                vmem((slots, width, hidden), BF16),
                vmem((slots, width, hidden), BF16),
                vmem((slots, hidden, width), BF16),
                vmem((width, out_cols), BF16),
                vmem((rows, width), F32),
                vmem((ep_n, 2, toks, quarter), BF16),
                vmem((ep_n, 2, toks, quarter), BF16),
                vmem((ep_n, toks, quarter), BF16),
                vmem((ep_n, toks, quarter), BF16),
                vmem((ep_n, toks, quarter), BF16),
                vmem((ep_n, toks, quarter), BF16),
                vmem((toks, width), BF16),
                dma((2, tp_n)),
                dma((2, ep_n)),
                dma((2, ep_n)),
                dma((2, ep_n)),
                dma((2, ep_n)),
                dma((2, ep_n)),
                dma((slots, 3)),
                dma((2, tp_n)),
                dma,
                dma((2, ep_n)),
                dma((2, ep_n)),
                dma((2, ep_n)),
                dma((2, tp_n)),
            ],
            compiler_params=pltpu.CompilerParams(
                collective_id=0, has_side_effects=True, vmem_limit_bytes=60 * 1024 * 1024
            ),
            cost_estimate=pl.CostEstimate(flops=work, bytes_accessed=6 * width * hidden * count, transcendentals=0),
        )(tokens, pack, w_latent, w_gate, w_up, w_out, w_restore)

    return jax.shard_map(
        shards,
        mesh=mesh,
        in_specs=(
            P(("groups", "ep"), "tp"),
            P(("groups", "ep"), None),
            P(("groups", "ep"), None),
            P("tp", None),
            P("ep", None, "tp"),
            P("ep", None, "tp"),
            P("ep", "tp", None),
            P("tp", None),
        ),
        out_specs=P(("groups", "ep"), "tp"),
        check_vma=False,
    )
```

time: 362 us -> 77.4 us (0.21)
  waiting for transfers between devices: 204 us -> 0 us
  Pallas kernels: 0 us -> 73.3 us
  blocking collectives: 52.9 us -> 0 us
  matrix products: 41.2 us -> 0 us
  local copies, waits for them, and re-layouts: 25.4 us -> 2.4 us
  other arithmetic: 20.1 us -> 1.4 us
  between operations: 13.2 us -> 0.01 us
  starting transfers between devices: 4.69 us -> 0 us
    reduce_scatter x3 -> x0, waiting for transfers between devices: 96.7 us -> none  [the longest x1 71.9 us: shards(): lax.psum_scatter(expert_part.astype(jnp.bfloat16), 'tp', scatter_dimensio...]
    pallas_call x0 -> x1, Pallas kernels: none -> 73.3 us  [shards(): pl.pallas_call(functools.partial(layer, ep_n, tp_n), out_shape=jax.ShapeD...]
    all_gather x1 -> x0, waiting for transfers between devices: 58.7 us -> none  [shards(): piece = lax.all_gather(arrived, 'tp', axis=2, tiled=True)]
    all_to_all x1 -> x0, blocking collectives: 52.9 us -> none  [shards(): lax.all_to_all(buffer.reshape(ep_count, exp_local * CAP, width), 'ep', sp...]
    all_to_all x1 -> x0, waiting for transfers between devices: 48.3 us -> none  [shards(): lax.all_to_all(expert_out.reshape(ep_count, exp_local * CAP, share), 'ep'...]
    dot_general x4 -> x0, matrix products: 41.2 us -> none  [the longest x1 20.9 us: shards(): jnp.einsum('sech,ehl->secl', hidden, w_out, preferred_element_type=jnp.fl...]
    another operation x3 -> x0, other arithmetic: 18.5 us -> none
    scatter x1 -> x0, local copies, waits for them, and re-layouts: 10.9 us -> none  [shards(): jnp.zeros((EXPERTS * CAP, width), jnp.bfloat16).at[slots].set(repeated)]
  transfers between devices with their start and end apart: 5 -> 0, of which waited for: 5 -> 0; matrix products, arithmetic and copies ran while one was open for 6% -> 0% of each run, Pallas kernels for 0% -> 0%
where the time goes in v2:
time: 77.4 us; the launch traced here: 77.1 us
  Pallas kernels  73.3 us (95%)
  local copies, waits for them, and re-layouts  2.4 us (3%)
  other arithmetic  1.4 us (2%)
    pallas_call x1, Pallas kernels, shards(): pl.pallas_call(functools.partial(layer, ep_n, tp_n), out_shape=jax.ShapeD...  73.3 us
    unnamed x1, local copies, waits for them, and re-layouts  1.67 us

profile of v2, /device:TPU:0, one launch (start us, length us, event | category | flops | bytes accessed | tf_op | source)
XLA Modules:
  0.0 77.1 jit_solution(7731601913331901962)
XLA Ops:
  0.0 0.7 convert_element_type.3
  0.7 0.7 pad_maximum_fusion
  1.4 0.7 copy.11.pack_ref
  2.1 73.3 %shard_map.82 = bf16[128,1024]{1,0:T(8,128)(2,1)} custom-call(bf16[128,1024]{1,0:T(8,128)(2,1)} %tok_ref.1, f32[128,32]{1,0:T(8,128)} %copy.11.pack_ref, bf16[1024,1024]{1,0:T(8,128)(2,1)} %wl_ref.1, bf16[16,1024,512]{2,1,0:T(8,128)(2,1)} %wg_hbm.1, bf16[16,1024,512]{2,1,0:T(8,128)(2,1)} %wu_hbm.1, bf16[16,512,1024]{2,1,0:T(8,128)(2,1)} %wo_hbm.1, ...), custom_call_target="tpu_custom_call" | custom-call | flops 25769803776 | bytes 50331648 | tf_op jit(solution)/shard_map/pallas_call | solution.py:230
  75.5 1.7 %copy.13 = bf16[128,1024]{1,0:T(8,128)(2,1)} copy(bf16[128,1024]{1,0:T(8,128)(2,1)} %shard_map.82) | data formatting | bytes 524288

commit v3 on v2

v3 whole, which is shorter than its diff:
```python
import functools

import jax
import jax.numpy as jnp
from jax import lax
from jax.experimental import pallas as pl
from jax.experimental.pallas import tpu as pltpu
from jax.sharding import PartitionSpec as P

F32, BF16 = jnp.float32, jnp.bfloat16
MESH = pl.DeviceIdType.MESH
SLOTS = 12


def remote(src, dst, send, recv, **where):
    return pltpu.make_async_remote_copy(
        src_ref=src, dst_ref=dst, send_sem=send, recv_sem=recv, device_id=where, device_id_type=MESH
    )


def layer(
    ep_n, tp_n, tok_ref, pack_ref, wl_ref, wg_hbm, wu_hbm, wo_hbm, wr_hbm, out_ref,
    p_send, p_recv, lat, pack, wg, wu, wo, wr, acc, r1_send, r1_recv, r2_send, r2_recv,
    r3_send, r3_recv, comb,
    p_sems, k_sems, a_sems, b1_sems, b2_sems, b3_sems, w_sems, wr_sems, own_sem,
    r1_sems, r2_sems, r3_sems, c_sems,
):
    ep, tp = lax.axis_index("ep"), lax.axis_index("tp")
    far = lax.rem(tp + 2, 4)
    near = tp + 1 - 2 * lax.rem(tp, 2)
    near_far = lax.rem(near + 2, 4)
    count = wg_hbm.shape[0]
    toks, top = tok_ref.shape[0], pack_ref.shape[1] // 2
    rows, width = lat.shape
    quarter = width // tp_n
    out_cols = out_ref.shape[1]
    unit = 2 if count % 2 == 0 else 1
    groups, held = count // unit, wg.shape[0] // unit
    half = ep_n // 2

    def cols(q):
        return pl.ds(pl.multiple_of(q * quarter, quarter), quarter)

    def block(d):
        return pl.ds(d * toks, toks)

    def after(d):
        return lax.rem(ep + d, ep_n)

    def loads(q):
        s = lax.rem(q, held) * unit
        return [
            pltpu.make_async_copy(hbm.at[q * unit + j], vmem.at[s + j], w_sems.at[s + j, i])
            for j in range(unit)
            for i, (hbm, vmem) in enumerate(((wg_hbm, wg), (wu_hbm, wu), (wo_hbm, wo)))
        ]

    def begin(q):
        for c in loads(q):
            c.start()

    early = min(held, 2)
    for q in range(early):
        begin(q)

    barrier = pltpu.get_barrier_semaphore()
    for d in range(1, ep_n):
        pl.semaphore_signal(barrier, inc=1, device_id={"ep": after(d)}, device_id_type=MESH)
    for d in range(1, tp_n):
        pl.semaphore_signal(barrier, inc=1, device_id={"tp": lax.rem(tp + d, tp_n)}, device_id_type=MESH)
    acc[...] = jnp.zeros_like(acc)
    pack[block(0), :] = pack_ref[...]
    pl.semaphore_wait(barrier, ep_n + tp_n - 2)

    def part(d):
        return remote(p_send.at[d], p_recv.at[d], p_sems.at[0, d], p_sems.at[1, d], tp=lax.rem(tp + d, tp_n))

    def packs(d):
        return remote(pack_ref, pack.at[block(d), :], k_sems.at[0, d], k_sems.at[1, d], ep=after(d))

    def spread(d):
        return remote(
            lat.at[block(0), cols(tp)], lat.at[block(d), cols(tp)], a_sems.at[0, d], a_sems.at[1, d], ep=after(d)
        )

    def b1(d):
        piece = lat.at[block(d), cols(tp)]
        return remote(piece, piece, b1_sems.at[0, d], b1_sems.at[1, d], tp=far)

    def b2(d):
        piece = lat.at[block(d), cols(tp)]
        return remote(piece, piece, b2_sems.at[0, d], b2_sems.at[1, d], tp=near)

    def b3(d):
        piece = lat.at[block(d), cols(far)]
        return remote(piece, piece, b3_sems.at[0, d], b3_sems.at[1, d], tp=near)

    def restore(d):
        peer = lax.rem(tp + d, tp_n)
        return remote(
            wr_hbm.at[:, pl.ds(pl.multiple_of(peer * out_cols, out_cols), out_cols)],
            wr.at[cols(tp), :], wr_sems.at[0, d], wr_sems.at[1, d], tp=peer,
        )

    own_restore = pltpu.make_async_copy(
        wr_hbm.at[:, pl.ds(pl.multiple_of(tp * out_cols, out_cols), out_cols)], wr.at[cols(tp), :], own_sem
    )

    def r1(d):
        return remote(r1_send.at[d], r1_recv.at[d], r1_sems.at[0, d], r1_sems.at[1, d], tp=near)

    def r2(d):
        return remote(r2_send.at[d], r2_recv.at[d], r2_sems.at[0, d], r2_sems.at[1, d], tp=far)

    def r3(d):
        return remote(r3_send.at[d], r3_recv.at[d], r3_sems.at[0, d], r3_sems.at[1, d], ep=after(ep_n - d))

    def gathered(d):
        piece = comb.at[:, cols(tp)]
        return remote(piece, piece, c_sems.at[0, d], c_sems.at[1, d], tp=lax.rem(tp + d, tp_n))

    first, second = list(range(half)), list(range(half, ep_n))

    for d in range(1, tp_n):
        w = wl_ref[:, cols(lax.rem(tp + d, tp_n))]
        p_send[d] = jnp.dot(tok_ref[...], w, preferred_element_type=F32).astype(BF16)
        part(d).start()
    mine = jnp.dot(tok_ref[...], wl_ref[:, cols(tp)], preferred_element_type=F32)
    for d in range(1, ep_n):
        packs(d).start()
    for d in range(1, tp_n):
        part(d).wait_recv()
        mine = mine + p_recv[d].astype(F32)
    lat[block(0), cols(tp)] = mine.astype(BF16)

    for d in range(1, ep_n):
        spread(d).start()

    def across(blocks):
        for d in blocks:
            if d:
                spread(d).wait_recv()
            b1(d).start()
            b2(d).start()

    def onward(blocks):
        for d in blocks:
            b1(d).wait_recv()
            b3(d).start()

    def arrived(blocks):
        for d in blocks:
            b2(d).wait_recv()
            b3(d).wait_recv()
            if d:
                packs(d).wait_recv()

    def sum_near(blocks):
        for d in blocks:
            r1_send[d, 0] = acc[block(d), cols(near)].astype(BF16)
            r1_send[d, 1] = acc[block(d), cols(near_far)].astype(BF16)
            r1(d).start()

    def sum_far(blocks):
        for d in blocks:
            r1(d).wait_recv()
            r2_send[d] = (acc[block(d), cols(far)] + r1_recv[d, 1].astype(F32)).astype(BF16)
            r2(d).start()

    def sum_ep(blocks):
        for d in blocks:
            r2(d).wait_recv()
            total = acc[block(d), cols(tp)] + r1_recv[d, 0].astype(F32) + r2_recv[d].astype(F32)
            if d:
                r3_send[d] = total.astype(BF16)
                r3(d).start()
            else:
                acc[block(d), cols(tp)] = total

    def exchange():
        for d in range(1, tp_n):
            restore(d).start()
        own_restore.start()

    across(first)
    for q in range(early, held):
        begin(q)
    onward(first)
    arrived(first)

    span = half * toks
    tile = min(span, 256)

    def experts(p, carry):
        back = p >= groups
        q = jnp.where(back, 2 * groups - 1 - p, p)
        base = jnp.where(back, span, 0)
        s = lax.rem(q, held) * unit

        @pl.when(jnp.logical_or(p < groups, q < groups - held))
        def _():
            for c in loads(q):
                c.wait()

        def tiles(i, inner):
            r = pl.ds(pl.multiple_of(base + i * tile, tile), tile)
            x = lat[r, :]
            chosen = pack[r, :]
            names, weights = chosen[:, :top], chosen[:, top:]
            hs = []
            for j in range(unit):
                name = (ep * count + q * unit + j).astype(F32)
                weight = jnp.sum(jnp.where(names == name, weights, 0.0), axis=1, keepdims=True)
                g = jnp.dot(x, wg[s + j], preferred_element_type=F32)
                u = jnp.dot(x, wu[s + j], preferred_element_type=F32)
                hs.append((g / (1.0 + jnp.exp(-g)) * u * weight).astype(BF16))
            total = acc[r, :]
            for j in range(unit):
                total = total + jnp.dot(hs[j], wo[s + j], preferred_element_type=F32)
            acc[r, :] = total
            return inner

        if span == tile:
            tiles(0, 0)
        else:
            lax.fori_loop(0, span // tile, tiles, 0)

        @pl.when(jnp.logical_and(p < groups, q + held < groups))
        def _():
            begin(q + held)

        @pl.when(jnp.logical_and(p >= groups, q >= held))
        def _():
            begin(q - held)

        last = groups - 1
        for when, what in (
            (0, lambda: across(second)),
            (min(1, last), lambda: onward(second)),
            (min(3, last), exchange),
            (last, lambda: arrived(second)),
            (last, lambda: sum_near(first)),
            (groups + min(1, last), lambda: sum_far(first)),
            (groups + min(3, last), lambda: sum_ep(first)),
        ):
            pl.when(p == when)(what)
        return carry

    lax.fori_loop(0, 2 * groups, experts, 0)

    sum_near(second)
    sum_far(second)
    sum_ep(second)
    total = acc[block(0), cols(tp)]
    for d in range(1, ep_n):
        r3(d).wait_recv()
        total = total + r3_recv[d].astype(F32)
    comb[:, cols(tp)] = total.astype(BF16)
    for d in range(1, tp_n):
        gathered(d).start()
    own_restore.wait()
    for d in range(1, tp_n):
        restore(d).wait_recv()
    for d in range(1, tp_n):
        gathered(d).wait_recv()
    out_ref[...] = jnp.dot(comb[...], wr[...], preferred_element_type=F32).astype(out_ref.dtype)
    for d in range(ep_n):
        for c in (b1, b2, b3, r1, r2):
            c(d).wait_send()
        if d:
            for c in (packs, spread, r3):
                c(d).wait_send()
    for d in range(1, tp_n):
        for c in (part, restore, gathered):
            c(d).wait_send()


def solution(mesh):
    ep_n, tp_n = mesh.shape["ep"], mesh.shape["tp"]

    def shards(tokens, routes, gates, w_latent, w_gate, w_up, w_out, w_restore):
        toks = tokens.shape[0]
        count, width, hidden = w_gate.shape
        rows, quarter = toks * ep_n, width // tp_n
        out_cols = w_restore.shape[1] // tp_n
        slots = min(SLOTS, count)
        pack = jnp.concatenate([routes.astype(F32), gates], axis=1)
        vmem, dma = pltpu.VMEM, pltpu.SemaphoreType.DMA
        in_vmem, in_hbm = pl.BlockSpec(memory_space=pltpu.VMEM), pl.BlockSpec(memory_space=pl.ANY)
        work = 6 * rows * width * hidden * count
        return pl.pallas_call(
            functools.partial(layer, ep_n, tp_n),
            out_shape=jax.ShapeDtypeStruct((toks, out_cols), BF16),
            in_specs=[in_vmem] * 3 + [in_hbm] * 4,
            out_specs=in_vmem,
            scratch_shapes=[
                vmem((tp_n, toks, quarter), BF16),
                vmem((tp_n, toks, quarter), BF16),
                vmem((rows, width), BF16),
                vmem((rows, pack.shape[1]), F32),
                vmem((slots, width, hidden), BF16),
                vmem((slots, width, hidden), BF16),
                vmem((slots, hidden, width), BF16),
                vmem((width, out_cols), BF16),
                vmem((rows, width), F32),
                vmem((ep_n, 2, toks, quarter), BF16),
                vmem((ep_n, 2, toks, quarter), BF16),
                vmem((ep_n, toks, quarter), BF16),
                vmem((ep_n, toks, quarter), BF16),
                vmem((ep_n, toks, quarter), BF16),
                vmem((ep_n, toks, quarter), BF16),
                vmem((toks, width), BF16),
                dma((2, tp_n)),
                dma((2, ep_n)),
                dma((2, ep_n)),
                dma((2, ep_n)),
                dma((2, ep_n)),
                dma((2, ep_n)),
                dma((slots, 3)),
                dma((2, tp_n)),
                dma,
                dma((2, ep_n)),
                dma((2, ep_n)),
                dma((2, ep_n)),
                dma((2, tp_n)),
            ],
            compiler_params=pltpu.CompilerParams(
                collective_id=0, has_side_effects=True, vmem_limit_bytes=60 * 1024 * 1024
            ),
            cost_estimate=pl.CostEstimate(flops=work, bytes_accessed=6 * width * hidden * count, transcendentals=0),
        )(tokens, pack, w_latent, w_gate, w_up, w_out, w_restore)

    return jax.shard_map(
        shards,
        mesh=mesh,
        in_specs=(
            P(("groups", "ep"), "tp"),
            P(("groups", "ep"), None),
            P(("groups", "ep"), None),
            P("tp", None),
            P("ep", None, "tp"),
            P("ep", None, "tp"),
            P("ep", "tp", None),
            P("tp", None),
        ),
        out_specs=P(("groups", "ep"), "tp"),
        check_vma=False,
    )
```

time: 77.4 us -> 87.6 us (1.13)
  Pallas kernels: 73.3 us -> 83.5 us
    pallas_call x1, Pallas kernels: 73.3 us -> 83.5 us  [shards(): pl.pallas_call(functools.partial(layer, ep_n, tp_n), out_shape=jax.ShapeD...]
where the time goes in v3:
time: 87.6 us; the launch traced here: 87.3 us
  Pallas kernels  83.5 us (95%)
  local copies, waits for them, and re-layouts  2.4 us (3%)
  other arithmetic  1.4 us (2%)
    pallas_call x1, Pallas kernels, shards(): pl.pallas_call(functools.partial(layer, ep_n, tp_n), out_shape=jax.ShapeD...  83.5 us

profile of v3, /device:TPU:0, one launch (start us, length us, event | category | flops | bytes accessed | tf_op | source)
XLA Modules:
  0.0 87.3 jit_solution(12442880856091806665)
XLA Ops:
  0.0 0.7 convert_element_type.3
  0.7 0.7 pad_maximum_fusion
  1.4 0.7 copy.11.pack_ref
  2.1 83.5 %shard_map.82 = bf16[128,1024]{1,0:T(8,128)(2,1)} custom-call(bf16[128,1024]{1,0:T(8,128)(2,1)} %tok_ref.1, f32[128,32]{1,0:T(8,128)} %copy.11.pack_ref, bf16[1024,1024]{1,0:T(8,128)(2,1)} %wl_ref.1, bf16[16,1024,512]{2,1,0:T(8,128)(2,1)} %wg_hbm.1, bf16[16,1024,512]{2,1,0:T(8,128)(2,1)} %wu_hbm.1, bf16[16,512,1024]{2,1,0:T(8,128)(2,1)} %wo_hbm.1, ...), custom_call_target="tpu_custom_call" | custom-call | flops 25769803776 | bytes 50331648 | tf_op jit(solution)/shard_map/pallas_call | solution.py:291
  85.6 1.7 %copy.13 = bf16[128,1024]{1,0:T(8,128)(2,1)} copy(bf16[128,1024]{1,0:T(8,128)(2,1)} %shard_map.82) | data formatting | bytes 524288

commit v4 on v2

--- a/solution.py
+++ b/solution.py
@@ -131,8 +131,9 @@
     own_restore.start()
 
     acc[...] = jnp.zeros_like(acc)
-    tile = min(rows, 256)
-    pair = min(rows // tile, 2)
+    tile = min(rows, 512)
+    hidden = wg.shape[2]
+    strip = hidden // 2
 
     def expert(e, carry):
         s = lax.rem(e, slots)
@@ -141,23 +142,26 @@
         name = (ep * count + e).astype(F32)
 
         def tiles(i, inner):
-            for j in range(pair):
-                r = pl.ds(pl.multiple_of((i * pair + j) * tile, tile), tile)
-                x = lat[r, :]
-                chosen = pack[r, :]
-                weight = jnp.sum(
-                    jnp.where(chosen[:, :top] == name, chosen[:, top:], 0.0), axis=1, keepdims=True
-                )
-                g = jnp.dot(x, wg[s], preferred_element_type=F32)
-                u = jnp.dot(x, wu[s], preferred_element_type=F32)
-                h = (g / (1.0 + jnp.exp(-g)) * u * weight).astype(BF16)
-                acc[r, :] += jnp.dot(h, wo[s], preferred_element_type=F32)
+            r = pl.ds(pl.multiple_of(i * tile, tile), tile)
+            x = lat[r, :]
+            chosen = pack[r, :]
+            weight = jnp.sum(
+                jnp.where(chosen[:, :top] == name, chosen[:, top:], 0.0), axis=1, keepdims=True
+            )
+            hs = []
+            for j in range(2):
+                cut = pl.ds(j * strip, strip)
+                g = jnp.dot(x, wg[s, :, cut], preferred_element_type=F32)
+                u = jnp.dot(x, wu[s, :, cut], preferred_element_type=F32)
+                hs.append((g / (1.0 + jnp.exp(-g)) * u * weight).astype(BF16))
+            h = jnp.concatenate(hs, axis=1)
+            acc[r, :] += jnp.dot(h, wo[s], preferred_element_type=F32)
             return inner
 
-        if rows == tile * pair:
+        if rows == tile:
             tiles(0, 0)
         else:
-            lax.fori_loop(0, rows // (tile * pair), tiles, 0)
+            lax.fori_loop(0, rows // tile, tiles, 0)
 
         @pl.when(e + slots < count)
         def _():

time: 77.4 us -> 74.8 us (0.966)
  Pallas kernels: 73.3 us -> 70.7 us
    pallas_call x1, Pallas kernels: 73.3 us -> 70.7 us  [shards(): pl.pallas_call(functools.partial(layer, ep_n, tp_n), out_shape=jax.ShapeD...]
where the time goes in v4:
time: 74.8 us; the launch traced here: 74.5 us
  Pallas kernels  70.7 us (95%)
  local copies, waits for them, and re-layouts  2.4 us (3%)
  other arithmetic  1.4 us (2%)
    pallas_call x1, Pallas kernels, shards(): pl.pallas_call(functools.partial(layer, ep_n, tp_n), out_shape=jax.ShapeD...  70.7 us
    unnamed x1, local copies, waits for them, and re-layouts  1.67 us

profile of v4, /device:TPU:0, one launch (start us, length us, event | category | flops | bytes accessed | tf_op | source)
XLA Modules:
  0.0 74.5 jit_solution(2402176928939184357)
XLA Ops:
  0.0 0.7 convert_element_type.3
  0.7 0.7 pad_maximum_fusion
  1.4 0.7 copy.11.pack_ref
  2.1 70.7 %shard_map.82 = bf16[128,1024]{1,0:T(8,128)(2,1)} custom-call(bf16[128,1024]{1,0:T(8,128)(2,1)} %tok_ref.1, f32[128,32]{1,0:T(8,128)} %copy.11.pack_ref, bf16[1024,1024]{1,0:T(8,128)(2,1)} %wl_ref.1, bf16[16,1024,512]{2,1,0:T(8,128)(2,1)} %wg_hbm.1, bf16[16,1024,512]{2,1,0:T(8,128)(2,1)} %wu_hbm.1, bf16[16,512,1024]{2,1,0:T(8,128)(2,1)} %wo_hbm.1, ...), custom_call_target="tpu_custom_call" | custom-call | flops 25769803776 | bytes 50331648 | tf_op jit(solution)/shard_map/pallas_call | solution.py:234
  72.8 1.7 %copy.13 = bf16[128,1024]{1,0:T(8,128)(2,1)} copy(bf16[128,1024]{1,0:T(8,128)(2,1)} %shard_map.82) | data formatting | bytes 524288

commit v5 on v4

--- a/solution.py
+++ b/solution.py
@@ -19,7 +19,7 @@
 
 
 def layer(
-    ep_n, tp_n, tok_ref, pack_ref, wl_ref, wg_hbm, wu_hbm, wo_hbm, wr_hbm, out_ref,
+    ep_n, tp_n, tok_ref, routes_ref, gates_ref, wl_ref, wg_hbm, wu_hbm, wo_hbm, wr_hbm, out_ref,
     p_send, p_recv, lat, pack, wg, wu, wo, wr, acc, r1_send, r1_recv, r2_send, r2_recv,
     r3_send, r3_recv, comb,
     p_sems, k_sems, a_sems, b1_sems, b2_sems, b3_sems, w_sems, wr_sems, own_sem,
@@ -31,7 +31,7 @@
     near_far = lax.rem(near + 2, 4)
     count = wg_hbm.shape[0]
     slots = wg.shape[0]
-    toks, top = tok_ref.shape[0], pack_ref.shape[1] // 2
+    toks, top = tok_ref.shape[0], routes_ref.shape[0]
     rows, width = lat.shape
     quarter = width // tp_n
     out_cols = out_ref.shape[1]
@@ -71,10 +71,11 @@
         sent.append(c)
     mine = jnp.dot(tok_ref[...], wl_ref[:, cols(tp)], preferred_element_type=F32)
     packs = [None]
-    pack[block(ep), :] = pack_ref[...]
+    fill = jnp.zeros((pack.shape[1] - 2 * top, toks), F32)
+    pack[block(ep), :] = jnp.concatenate([routes_ref[...].astype(F32), gates_ref[...], fill], axis=0).T
     for d in range(1, ep_n):
         c = remote(
-            pack_ref, pack.at[block(ep), :], k_sems.at[0, d], k_sems.at[1, d], ep=lax.rem(ep + d, ep_n)
+            pack.at[block(ep), :], pack.at[block(ep), :], k_sems.at[0, d], k_sems.at[1, d], ep=lax.rem(ep + d, ep_n)
         )
         c.start()
         packs.append(c)
@@ -146,7 +147,7 @@
             x = lat[r, :]
             chosen = pack[r, :]
             weight = jnp.sum(
-                jnp.where(chosen[:, :top] == name, chosen[:, top:], 0.0), axis=1, keepdims=True
+                jnp.where(chosen[:, :top] == name, chosen[:, top : 2 * top], 0.0), axis=1, keepdims=True
             )
             hs = []
             for j in range(2):
@@ -211,9 +212,12 @@
     own_restore.wait()
     for c in restore:
         c.wait_recv()
-    for c in gathered:
-        c.wait_recv()
-    out_ref[...] = jnp.dot(comb[...], wr[...], preferred_element_type=F32).astype(out_ref.dtype)
+    result = jnp.dot(comb[:, cols(tp)], wr[cols(tp), :], preferred_element_type=F32)
+    for d in range(1, tp_n):
+        gathered[d - 1].wait_recv()
+        peer = lax.rem(tp + tp_n - d, tp_n)
+        result = result + jnp.dot(comb[:, cols(peer)], wr[cols(peer), :], preferred_element_type=F32)
+    out_ref[...] = result.astype(out_ref.dtype)
     for c in sent:
         c.wait_send()
 
@@ -227,20 +231,20 @@
         rows, quarter = toks * ep_n, width // tp_n
         out_cols = w_restore.shape[1] // tp_n
         slots = min(SLOTS, count)
-        pack = jnp.concatenate([routes.astype(F32), gates], axis=1)
+        lanes = -(-2 * routes.shape[1] // 128) * 128
         vmem, dma = pltpu.VMEM, pltpu.SemaphoreType.DMA
         in_vmem, in_hbm = pl.BlockSpec(memory_space=pltpu.VMEM), pl.BlockSpec(memory_space=pl.ANY)
         work = 6 * rows * width * hidden * count
         return pl.pallas_call(
             functools.partial(layer, ep_n, tp_n),
             out_shape=jax.ShapeDtypeStruct((toks, out_cols), BF16),
-            in_specs=[in_vmem] * 3 + [in_hbm] * 4,
+            in_specs=[in_vmem] * 4 + [in_hbm] * 4,
             out_specs=in_vmem,
             scratch_shapes=[
                 vmem((tp_n, toks, quarter), BF16),
                 vmem((tp_n, toks, quarter), BF16),
                 vmem((rows, width), BF16),
-                vmem((rows, pack.shape[1]), F32),
+                vmem((rows, lanes), F32),
                 vmem((slots, width, hidden), BF16),
                 vmem((slots, width, hidden), BF16),
                 vmem((slots, hidden, width), BF16),
@@ -271,7 +275,7 @@
                 collective_id=0, has_side_effects=True, vmem_limit_bytes=60 * 1024 * 1024
             ),
             cost_estimate=pl.CostEstimate(flops=work, bytes_accessed=6 * width * hidden * count, transcendentals=0),
-        )(tokens, pack, w_latent, w_gate, w_up, w_out, w_restore)
+        )(tokens, routes.T, gates.T, w_latent, w_gate, w_up, w_out, w_restore)
 
     return jax.shard_map(
         shards,

time: 74.8 us -> 72.6 us (0.971)
  other arithmetic: 1.4 us -> 0 us
where the time goes in v5:
time: 72.6 us; the launch traced here: 72.4 us
  Pallas kernels  70.7 us (97%)
  local copies, waits for them, and re-layouts  1.67 us (2%)
    pallas_call x1, Pallas kernels, shards(): pl.pallas_call(functools.partial(layer, ep_n, tp_n), out_shape=jax.ShapeD...  70.7 us
    unnamed x1, local copies, waits for them, and re-layouts  1.67 us

profile of v5, /device:TPU:0, one launch (start us, length us, event | category | flops | bytes accessed | tf_op | source)
XLA Modules:
  0.0 72.4 jit_solution(8870473031011969717)
XLA Ops:
  0.0 70.7 %shard_map.82 = bf16[128,1024]{1,0:T(8,128)(2,1)} custom-call(bf16[128,1024]{1,0:T(8,128)(2,1)} %tok_ref.1, s32[16,128]{1,0:T(8,128)} %bitcast.2, f32[16,128]{1,0:T(8,128)} %bitcast.3, bf16[1024,1024]{1,0:T(8,128)(2,1)} %wl_ref.1, bf16[16,1024,512]{2,1,0:T(8,128)(2,1)} %wg_hbm.1, bf16[16,1024,512]{2,1,0:T(8,128)(2,1)} %wu_hbm.1, ...), custom_call_target="tpu_custom_call" | custom-call | flops 25769803776 | bytes 50331648 | tf_op jit(solution)/shard_map/pallas_call | solution.py:238
  70.7 1.7 %copy.10 = bf16[128,1024]{1,0:T(8,128)(2,1)} copy(bf16[128,1024]{1,0:T(8,128)(2,1)} %shard_map.82) | data formatting | bytes 524288
